TPU v7x, 32 devices: a whole 2x2x4 slice. The times are simulated.
32 devices in a mesh: groups: 2 (over x), gx: 8 (over z, y), gy: 2 (over core).
Axes of the slice: x: 2, y: 2, z: 4, core: 2. Of those that a mesh axis runs over, the one named last changes fastest.
Arguments:
- saved_preact: bfloat16 [2048, 49152], P(('groups', 'gy'), 'gx'), parts along dimension 0, may hold values from -6 to 6
- output_grad: bfloat16 [2048, 7424], P(('groups', 'gx'), 'gy'), parts along dimension 0, may hold values from -0.75 to 0.75
- down_weight: bfloat16 [49152, 7424], P('gx', 'gy'), may hold values from -0.5 to 0.5
Outputs:
- preact_grad: bfloat16 [2048, 49152], P(('groups', 'gy'), 'gx'), parts along dimension 0
- weight_grad: bfloat16 [98304, 7424], P(('groups', 'gx'), 'gy'), parts along dimension 0
There are 2 independent parts, one for each index of `groups`. A program takes and returns all parts, laid end to end along the dimension named above; an argument that names none is the same for every part. Nothing has to cross between parts.
All inputs are finite; a program needn't handle non-finite values.
Results may differ from a plain program's by a relative error of at most 0.0051.
Values may be sent and summed in bfloat16 or wider, within the bound.
A program may use at most 256 MiB of HBM per device.

v0:
```python
import jax
import jax.numpy as jnp
from jax import lax
from jax.sharding import PartitionSpec as P


def gelu_value(values):
    return values * 0.5 * (1.0 + jax.scipy.special.erf(values * 0.7071067811865476))


def gelu_slope(values):
    cumulative = 0.5 * (1.0 + jax.scipy.special.erf(values * 0.7071067811865476))
    density = jnp.exp(-0.5 * values * values) * 0.3989422804014327
    return cumulative + values * density


def body(saved_preact, output_grad, down_weight):
    preact = saved_preact.astype(jnp.float32)
    own_activation = gelu_value(preact).astype(jnp.bfloat16)
    activations = lax.all_gather(own_activation, "gy", axis=0, tiled=True)
    gathered = lax.all_gather(output_grad, "gx", axis=0, tiled=True)
    partial_value = lax.dot_general(
        gathered, down_weight, (((1,), (1,)), ((), ())), preferred_element_type=jnp.float32
    )
    hidden_grad = lax.psum_scatter(partial_value, "gy", scatter_dimension=0, tiled=True)
    preact_grad = (hidden_grad * gelu_slope(preact)).astype(jnp.bfloat16)
    weight_grad = lax.dot_general(
        activations, gathered, (((0,), (0,)), ((), ())), preferred_element_type=jnp.float32
    )
    return (preact_grad, weight_grad.astype(jnp.bfloat16))


def solution(mesh):
    return jax.shard_map(
        body,
        mesh=mesh,
        in_specs=(P(("groups", "gy"), "gx"), P(("groups", "gx"), "gy"), P("gx", "gy")),
        out_specs=(P(("groups", "gy"), "gx"), P(("groups", "gx"), "gy")),
        check_vma=False,
    )
```

profile of v0, /device:TPU:0, one launch (start us, length us, event | category | flops | bytes accessed | tf_op | source)
XLA Modules:
  0.0 323.9 jit_solution(10621178158444476358)
XLA Ops:
  7.2 0.0 all-gather.3.cloned.1.call-start
  7.2 0.7 all-gather.3.cloned.1.call-update
  7.9 0.0 reduce-scatter.2.cloned.1.call-start
  7.9 120.2 %all-gather.3.cloned.1.call-done = bf16[1024,3712]{1,0:T(8,128)(2,1)} async-done(((bf16[128,3712]{1,0:T(8,128)(2,1)}), bf16[1024,3712]{1,0:T(8,128)(2,1)}) %all-gather.3.cloned.1.call-update) | async-done | bytes 7602192 | tf_op jit(solution)/shard_map/all_gather | solution.py:21
  128.1 57.2 %fusion.9 = f32[1024,6144]{1,0:T(8,128)} fusion(bf16[1024,3712]{1,0:T(8,128)(2,1)} %all-gather.3.cloned.1.call-done, bf16[6144,3712]{1,0:T(8,128)(2,1)} %param.5), kind=kOutput, calls=%fused_computation.15 | convolution fusion | flops 46707769344 | bytes 78381056 | tf_op jit(solution)/shard_map/dot_general | solution.py:22
  185.3 0.0 reduce-scatter.2.cloned.1.call-update
  185.3 0.0 all-gather.5.cloned.1.call-start
  185.4 33.7 %reduce-scatter.2.cloned.1.call-done = f32[512,6144]{1,0:T(8,128)} async-done(((f32[1024,6144]{1,0:T(8,128)}), f32[512,6144]{1,0:T(8,128)}) %reduce-scatter.2.cloned.1.call-update) | async-done | bytes 12582928 | tf_op jit(solution)/shard_map/reduce_scatter | solution.py:25
  219.1 13.5 %fusion.8 = (bf16[512,6144]{1,0:T(8,128)(2,1)}, bf16[512,6144]{1,0:T(8,128)(2,1)}) fusion(bf16[512,6144]{1,0:T(8,128)(2,1)} %param.3, f32[512,6144]{1,0:T(8,128)} %reduce-scatter.2.cloned.1.call-done), kind=kLoop, calls=%fused_computation.14 | loop fusion | flops 44040192 | bytes 31457280 | tf_op jit(solution)/shard_map/convert_element_type | solution.py:19
  232.6 0.0 all-gather.5.cloned.1.call-update
  232.6 26.2 %all-gather.5.cloned.1.call-done = bf16[1024,6144]{1,0:T(8,128)(2,1)} async-done(((bf16[512,6144]{1,0:T(8,128)(2,1)}), bf16[1024,6144]{1,0:T(8,128)(2,1)}) %all-gather.5.cloned.1.call-update) | async-done | bytes 12582928 | tf_op jit(solution)/shard_map/all_gather | solution.py:20
  258.9 58.5 %convolution_convert_fusion = bf16[6144,3712]{1,0:T(8,128)(2,1)} fusion(bf16[1024,6144]{1,0:T(8,128)(2,1)} %all-gather.5.cloned.1.call-done, bf16[1024,3712]{1,0:T(8,128)(2,1)} %all-gather.3.cloned.1.call-done), kind=kOutput, calls=%fused_computation | convolution fusion | flops 46730575872 | bytes 65798144 | tf_op jit(solution)/shard_map/dot_general | solution.py:27
Async XLA Ops:
  7.2 121.0 %all-gather.3.cloned.1.call-start = ((), (), s32[]{:S(2)}) async-start(), calls=%async_computation.1 | async-start | bytes 8552448 | tf_op jit(solution)/shard_map/all_gather | solution.py:21
  7.9 211.2 %reduce-scatter.2.cloned.1.call-start = ((), (), s32[]{:S(2)}) async-start(), calls=%async_computation.2 | async-start | bytes 37748736 | tf_op jit(solution)/shard_map/reduce_scatter | solution.py:25
  185.3 73.5 %all-gather.5.cloned.1.call-start = ((), (), s32[]{:S(2)}) async-start(), calls=%async_computation.3 | async-start | bytes 18874368 | tf_op jit(solution)/shard_map/all_gather | solution.py:20
Sparse Core Ops, SparseCore 0:
  10.2 117.8 all-gather.2
  185.4 33.6 reduce-scatter.1
  232.8 26.0 all-gather.4
where the time goes:
time: 324 us
  waiting for transfers between devices  181 us (56%)
  matrix products  116 us (36%)
  between operations  13.7 us (4%)
  other arithmetic  13.5 us (4%)
    all_gather x1, waiting for transfers between devices, body(): gathered = lax.all_gather(output_grad, 'gx', axis=0, tiled=True)  120 us
    dot_general x1, matrix products, body(): lax.dot_general(activations, gathered, (((0,), (0,)), ((), ())), preferre...  58.5 us
    dot_general x1, matrix products, body(): lax.dot_general(gathered, down_weight, (((1,), (1,)), ((), ())), preferre...  57.2 us
    reduce_scatter x1, waiting for transfers between devices, body(): lax.psum_scatter(partial_value, 'gy', scatter_dimension=0, tiled=True)  33.7 us
    all_gather x1, waiting for transfers between devices, body(): activations = lax.all_gather(own_activation, 'gy', axis=0, tiled=True)  26.2 us
    convert_element_type x1, other arithmetic, body(): own_activation = gelu_value(preact).astype(jnp.bfloat16)  13.5 us
  transfers between devices with their start and end apart: 3, of which 3 were waited for; matrix products, arithmetic and copies ran while one was open for 0% of the time, Pallas kernels for 0%

commit v1 on v0

v1 whole, which is shorter than its diff:
```python
import functools

import jax
import jax.numpy as jnp
from jax import lax
from jax.experimental import pallas as pl
from jax.experimental.pallas import tpu as pltpu
from jax.sharding import PartitionSpec as P

MESH = pl.DeviceIdType.MESH
VMEM_BYTES = 60 * 1024 * 1024
STAGES = 4


def gelu_value(values):
    return values * 0.5 * (1.0 + lax.erf(values * 0.7071067811865476))


def gelu_slope(values):
    cumulative = 0.5 * (1.0 + lax.erf(values * 0.7071067811865476))
    density = jnp.exp(-0.5 * values * values) * 0.3989422804014327
    return cumulative + values * density


def pick_tile(extent):
    return next(tile for tile in (512, 384, 256, 128) if extent % tile == 0)


def gather_kernel(outer, inner, tile, preact, grad, weight, act_out, grad_out, part_own, part_peer,
                  weight_v, grad_v, pre_v, act_v, part_v,
                  weight_sem, own_sem, out_sem, send_sem, recv_sem, pre_sem, act_sem, act_send, act_recv,
                  part_sem, part_send, part_recv):
    me, core = lax.axis_index("gx"), lax.axis_index("gy")
    row, col = me // inner, me % inner
    peer = 1 - core
    shard = grad.shape[0]
    half, hidden = preact.shape
    tiles = hidden // tile
    chunk = shard * inner
    per_half = outer // 2
    up, down = row + 1 < outer, row >= 1
    east, west = col + 1 < inner, col >= 1
    exists = (up, down, east, west)
    target = (me + inner, me - inner, me + 1, me - 1)

    def rows_of(index):
        return pl.ds(pl.multiple_of(index * shard, shard), shard)

    def shard_copy(index, way, src=None):
        place = grad_v.at[rows_of(index)]
        return pltpu.make_async_remote_copy(
            src_ref=place if src is None else src, dst_ref=place,
            send_sem=send_sem.at[way, index], recv_sem=recv_sem.at[index],
            device_id={"gx": target[way]}, device_id_type=MESH)

    def wait_shard(index):
        place = grad_v.at[rows_of(index)]
        pltpu.make_async_remote_copy(
            src_ref=place, dst_ref=place, send_sem=send_sem.at[0, index], recv_sem=recv_sem.at[index],
            device_id={"gx": me}, device_id_type=MESH).wait_recv()

    def send(index, way, src=None):
        @pl.when(exists[way])
        def _():
            shard_copy(index, way, src).start()

    def weight_copy(n):
        rows = pl.ds(pl.multiple_of(n * tile, tile), tile)
        return pltpu.make_async_copy(weight.at[rows], weight_v.at[rows], weight_sem.at[n])

    barrier = pltpu.get_barrier_semaphore()
    for way in range(4):
        @pl.when(exists[way])
        def _():
            pl.semaphore_signal(barrier, inc=1, device_id={"gx": target[way]}, device_id_type=MESH)
    pl.semaphore_signal(barrier, inc=1, device_id={"gy": peer}, device_id_type=MESH)
    count = 1 + sum(jnp.where(e, 1, 0) for e in exists)
    pl.semaphore_wait(barrier, count)

    for way in (2, 3, 0, 1):
        send(me, way, grad)
    own = pltpu.make_async_copy(grad, grad_v.at[rows_of(me)], own_sem)
    own.start()

    def pre_copy(n):
        cols = pl.ds(pl.multiple_of(n * tile, tile), tile)
        return pltpu.make_async_copy(preact.at[:, cols], pre_v.at[n % 2], pre_sem.at[n % 2])

    pre_copy(0).start()

    @pl.loop(0, tiles)
    def _(n):
        weight_copy(n).start()

    own_rows = pl.ds(pl.multiple_of(core * half, half), half)

    def act_copies(n):
        cols = pl.ds(pl.multiple_of(n * tile, tile), tile)
        place = act_out.at[own_rows, cols]
        here = pltpu.make_async_copy(act_v.at[n % 2], place, act_sem.at[n % 2])
        there = pltpu.make_async_remote_copy(
            src_ref=act_v.at[n % 2], dst_ref=place, send_sem=act_send.at[n % 2], recv_sem=act_recv,
            device_id={"gy": peer}, device_id_type=MESH)
        return here, there

    @pl.loop(0, tiles)
    def _(n):
        pre_copy(n).wait()

        @pl.when(n + 1 < tiles)
        def _():
            pre_copy(n + 1).start()

        @pl.when(n >= 2)
        def _():
            here, there = act_copies(n - 2)
            here.wait()
            there.wait_send()

        @pl.loop(0, half // 32)
        def _(s):
            strip = pl.ds(pl.multiple_of(s * 32, 32), 32)
            values = pre_v[n % 2, strip, :].astype(jnp.float32)
            act_v[n % 2, strip, :] = gelu_value(values).astype(jnp.bfloat16)

        here, there = act_copies(n)
        here.start()
        there.start()

    @pl.loop(max(tiles - 2, 0), tiles)
    def _(n):
        here, there = act_copies(n)
        here.wait()
        there.wait_send()

    own.wait()

    near = jnp.minimum(row, outer - 1 - row)

    def chunk_at(k):
        zigzag = jnp.where(k % 2 == 1, row - (k + 1) // 2, row + k // 2)
        rest = jnp.where(row <= outer - 1 - row, k, outer - 1 - k)
        return jnp.where(k <= 2 * near, zigzag, rest)

    def grad_back(c):
        rows = pl.ds(pl.multiple_of(c * chunk, chunk), chunk)
        return pltpu.make_async_copy(grad_v.at[rows], grad_out.at[rows], out_sem.at[c])

    @pl.loop(0, outer)
    def _(k):
        far = k + 1

        @pl.when(row >= far)
        def _():
            index = (row - far) * inner + col
            wait_shard(index)
            send(index, 0)
            send(index, 2)
            send(index, 3)

        @pl.when(row + far < outer)
        def _():
            index = (row + far) * inner + col
            wait_shard(index)
            send(index, 1)
            send(index, 2)
            send(index, 3)

        c = chunk_at(k)

        @pl.loop(1, inner)
        def _(e):
            @pl.when(col >= e)
            def _():
                index = c * inner + col - e
                wait_shard(index)
                send(index, 2)

            @pl.when(col + e < inner)
            def _():
                index = c * inner + col + e
                wait_shard(index)
                send(index, 3)

        grad_back(c).start()
        mine = c // per_half == core
        rows = pl.ds(pl.multiple_of(c * chunk, chunk), chunk)
        part_rows = pl.ds(pl.multiple_of(c % per_half * chunk, chunk), chunk)

        def to_own(n):
            cols = pl.ds(pl.multiple_of(n * tile, tile), tile)
            return pltpu.make_async_copy(
                part_v.at[n % STAGES], part_own.at[part_rows, cols], part_sem.at[n % STAGES])

        def to_peer(n):
            cols = pl.ds(pl.multiple_of(n * tile, tile), tile)
            return pltpu.make_async_remote_copy(
                src_ref=part_v.at[n % STAGES], dst_ref=part_peer.at[part_rows, cols],
                send_sem=part_send.at[n % STAGES], recv_sem=part_recv,
                device_id={"gy": peer}, device_id_type=MESH)

        def drain(n):
            @pl.when(mine)
            def _():
                to_own(n).wait()

            @pl.when(jnp.logical_not(mine))
            def _():
                to_peer(n).wait_send()

        @pl.loop(0, tiles)
        def _(n):
            @pl.when(k == 0)
            def _():
                weight_copy(n).wait()

            @pl.when(n >= STAGES)
            def _():
                drain(n - STAGES)

            part = lax.dot_general(
                grad_v[rows, :], weight_v[pl.ds(pl.multiple_of(n * tile, tile), tile), :],
                (((1,), (1,)), ((), ())), preferred_element_type=jnp.float32)
            part_v[n % STAGES] = part.astype(jnp.bfloat16)

            @pl.when(mine)
            def _():
                to_own(n).start()

            @pl.when(jnp.logical_not(mine))
            def _():
                to_peer(n).start()

        @pl.loop(max(tiles - STAGES, 0), tiles)
        def _(n):
            drain(n)

    @pl.loop(0, outer)
    def _(c):
        grad_back(c).wait()
        line = c * inner + col

        @pl.when(jnp.logical_and(up, c <= row))
        def _():
            shard_copy(line, 0).wait_send()

        @pl.when(jnp.logical_and(down, c >= row))
        def _():
            shard_copy(line, 1).wait_send()

        @pl.loop(0, inner)
        def _(e):
            @pl.when(jnp.logical_and(east, e <= col))
            def _():
                shard_copy(c * inner + e, 2).wait_send()

            @pl.when(jnp.logical_and(west, e >= col))
            def _():
                shard_copy(c * inner + e, 3).wait_send()

    peer_rows = act_out.at[pl.ds(pl.multiple_of(peer * half, half), half)]
    pltpu.make_async_remote_copy(
        src_ref=peer_rows, dst_ref=peer_rows, send_sem=act_send.at[0], recv_sem=act_recv,
        device_id={"gy": peer}, device_id_type=MESH).wait_recv()
    pltpu.make_async_remote_copy(
        src_ref=part_peer, dst_ref=part_peer, send_sem=part_send.at[0], recv_sem=part_recv,
        device_id={"gy": peer}, device_id_type=MESH).wait_recv()


def gather_call(inner, parts, preact, grad, weight):
    half, hidden = preact.shape
    shard, features = grad.shape
    outer = parts // inner
    tile = pick_tile(hidden)
    tokens = shard * parts
    any_spec = pl.BlockSpec(memory_space=pl.ANY)
    return pl.pallas_call(
        functools.partial(gather_kernel, outer, inner, tile),
        out_shape=(
            jax.ShapeDtypeStruct((tokens, hidden), jnp.bfloat16),
            jax.ShapeDtypeStruct((tokens, features), jnp.bfloat16),
            jax.ShapeDtypeStruct((half, hidden), jnp.bfloat16),
            jax.ShapeDtypeStruct((half, hidden), jnp.bfloat16),
        ),
        in_specs=[any_spec] * 3,
        out_specs=(any_spec,) * 4,
        scratch_shapes=[
            pltpu.VMEM((hidden, features), jnp.bfloat16),
            pltpu.VMEM((tokens, features), jnp.bfloat16),
            pltpu.VMEM((2, half, tile), jnp.bfloat16),
            pltpu.VMEM((2, half, tile), jnp.bfloat16),
            pltpu.VMEM((STAGES, shard * inner, tile), jnp.bfloat16),
            pltpu.SemaphoreType.DMA((hidden // tile,)),
            pltpu.SemaphoreType.DMA,
            pltpu.SemaphoreType.DMA((outer,)),
            pltpu.SemaphoreType.DMA((4, parts)),
            pltpu.SemaphoreType.DMA((parts,)),
            pltpu.SemaphoreType.DMA((2,)),
            pltpu.SemaphoreType.DMA((2,)),
            pltpu.SemaphoreType.DMA((2,)),
            pltpu.SemaphoreType.DMA,
            pltpu.SemaphoreType.DMA((STAGES,)),
            pltpu.SemaphoreType.DMA((STAGES,)),
            pltpu.SemaphoreType.DMA,
        ],
        compiler_params=pltpu.CompilerParams(
            collective_id=0, has_side_effects=True, vmem_limit_bytes=VMEM_BYTES),
        cost_estimate=pl.CostEstimate(
            flops=2 * tokens * hidden * features, bytes_accessed=2 * hidden * features,
            transcendentals=half * hidden),
        name="gather_hidden_grad",
    )(preact, grad, weight)


def weight_kernel(act, grad, preact, part_own, part_peer, weight_grad, preact_grad):
    turned = act[...].T
    features = grad.shape[1]
    for start in range(0, features, 1024):
        cols = slice(start, min(start + 1024, features))
        weight_grad[:, cols] = jnp.dot(
            turned, grad[:, cols], preferred_element_type=jnp.float32).astype(jnp.bfloat16)

    @pl.loop(0, preact.shape[0] // 32)
    def _(s):
        strip = pl.ds(pl.multiple_of(s * 32, 32), 32)
        total = part_own[strip, :].astype(jnp.float32) + part_peer[strip, :].astype(jnp.float32)
        slope = gelu_slope(preact[strip, :].astype(jnp.float32))
        preact_grad[strip, :] = (total * slope).astype(jnp.bfloat16)


def weight_call(act, grad, preact, part_own, part_peer):
    tokens, hidden = act.shape
    features = grad.shape[1]
    half = preact.shape[0]
    tile = pick_tile(hidden)
    block = pl.BlockSpec((half, tile), lambda i: (0, i))
    return pl.pallas_call(
        weight_kernel,
        grid=(hidden // tile,),
        out_shape=(
            jax.ShapeDtypeStruct((hidden, features), jnp.bfloat16),
            jax.ShapeDtypeStruct((half, hidden), jnp.bfloat16),
        ),
        in_specs=[
            pl.BlockSpec((tokens, tile), lambda i: (0, i)),
            pl.BlockSpec((tokens, features), lambda i: (0, 0), pipeline_mode=pl.Buffered(1)),
            block, block, block,
        ],
        out_specs=(pl.BlockSpec((tile, features), lambda i: (i, 0)), block),
        compiler_params=pltpu.CompilerParams(vmem_limit_bytes=VMEM_BYTES),
        cost_estimate=pl.CostEstimate(
            flops=2 * tokens * hidden * features, bytes_accessed=2 * hidden * features,
            transcendentals=2 * half * hidden),
        name="weight_grad",
    )(act, grad, preact, part_own, part_peer)


def solution(mesh):
    parts = mesh.shape["gx"]
    inner = 2 ** ((parts.bit_length() - 1) // 2)

    def body(saved_preact, output_grad, down_weight):
        act, grad, part_own, part_peer = gather_call(inner, parts, saved_preact, output_grad, down_weight)
        weight_grad, preact_grad = weight_call(act, grad, saved_preact, part_own, part_peer)
        return preact_grad, weight_grad

    return jax.shard_map(
        body,
        mesh=mesh,
        in_specs=(P(("groups", "gy"), "gx"), P(("groups", "gx"), "gy"), P("gx", "gy")),
        out_specs=(P(("groups", "gy"), "gx"), P(("groups", "gx"), "gy")),
        check_vma=False,
    )
```

time: 324 us -> 180 us (0.56)
  waiting for transfers between devices: 181 us -> 0 us
  Pallas kernels: 0 us -> 179 us
  matrix products: 116 us -> 0 us
  other arithmetic: 13.5 us -> 0 us
  between operations: 13.7 us -> 0.64 us
    pallas_call x0 -> x2, Pallas kernels: none -> 179 us  [the longest x1 112 us: gather_call(): pl.pallas_call(functools.partial(gather_kernel, outer, inner, tile), out_...]
    all_gather x2 -> x0, waiting for transfers between devices: 146 us -> none  [the longest x1 120 us: body(): gathered = lax.all_gather(output_grad, 'gx', axis=0, tiled=True)]
    dot_general x2 -> x0, matrix products: 116 us -> none  [the longest x1 58.5 us: body(): lax.dot_general(activations, gathered, (((0,), (0,)), ((), ())), preferre...]
    reduce_scatter x1 -> x0, waiting for transfers between devices: 33.7 us -> none  [body(): lax.psum_scatter(partial_value, 'gy', scatter_dimension=0, tiled=True)]
    convert_element_type x1 -> x0, other arithmetic: 13.5 us -> none  [body(): own_activation = gelu_value(preact).astype(jnp.bfloat16)]
  transfers between devices with their start and end apart: 3 -> 0, of which waited for: 3 -> 0; matrix products, arithmetic and copies ran while one was open for 0% -> 0% of each run, Pallas kernels for 0% -> 0%
where the time goes in v1:
time: 180 us; the launch traced here: 179 us
  Pallas kernels  179 us (99%)
    pallas_call x1, Pallas kernels, gather_call(): pl.pallas_call(functools.partial(gather_kernel, outer, inner, tile), out_...  112 us
    pallas_call x1, Pallas kernels, weight_call(): pl.pallas_call(weight_kernel, grid=(hidden // tile,), out_shape=(jax.Shap...  66.4 us

profile of v1, /device:TPU:0, one launch (start us, length us, event | category | flops | bytes accessed | tf_op | source)
XLA Modules:
  0.0 179.3 jit_solution(9175838729166738072)
XLA Ops:
  0.6 112.3 %gather_hidden_grad.1 = (bf16[1024,6144]{1,0:T(8,128)(2,1)}, bf16[1024,3712]{1,0:T(8,128)(2,1)}, bf16[512,6144]{1,0:T(8,128)(2,1)}, bf16[512,6144]{1,0:T(8,128)(2,1)}) custom-call(bf16[512,6144]{1,0:T(8,128)(2,1)} %preact.3, bf16[128,3712]{1,0:T(8,128)(2,1)} %grad.1, bf16[6144,3712]{1,0:T(8,128)(2,1)} %weight.1), custom_call_target="tpu_custom_call" | custom-call | flops 46707769344 | bytes 45613056 | tf_op jit(solution)/shard_map/gather_hidden_grad/pallas_call | solution.py:277
  113.0 66.4 %weight_grad.1 = (bf16[6144,3712]{1,0:T(8,128)(2,1)}, bf16[512,6144]{1,0:T(8,128)(2,1)}) custom-call(bf16[1024,6144]{1,0:T(8,128)(2,1)} %get-tuple-element.8.act, bf16[1024,3712]{1,0:T(8,128)(2,1)} %get-tuple-element.9.grad, bf16[512,6144]{1,0:T(8,128)(2,1)} %preact.3, bf16[512,6144]{1,0:T(8,128)(2,1)} %get-tuple-element.10.part_own, ...), custom_call_target="tpu_custom_call" | custom-call | flops 46707769344 | bytes 45613056 | tf_op jit(solution)/shard_map/weight_grad/pallas_call | solution.py:337

commit v2 on v1

v2 whole, which is shorter than its diff:
```python
import functools

import jax
import jax.numpy as jnp
from jax import lax
from jax.experimental import pallas as pl
from jax.experimental.pallas import tpu as pltpu
from jax.sharding import PartitionSpec as P

MESH = pl.DeviceIdType.MESH
VMEM_BYTES = 60 * 1024 * 1024
STAGES = 2


def pick_tile(extent, most):
    return next(tile for tile in (1024, 768, 512, 384, 256, 128) if tile <= most and extent % tile == 0)


def gather_kernel(outer, inner, tile, small, preact, grad, weight,
                  act_out, slope_out, grad_out, part_own, part_peer,
                  weight_v, grad_v, pre_v, act_v, slope_v, part_v,
                  weight_sem, own_sem, out_sem, send_sem, recv_sem, pre_sem, act_sem, slope_sem, act_send, act_recv,
                  part_sem, part_send, part_recv):
    me, core = lax.axis_index("gx"), lax.axis_index("gy")
    row, col = me // inner, me % inner
    peer = 1 - core
    shard = grad.shape[0]
    half, hidden = preact.shape
    tiles, smalls = hidden // tile, hidden // small
    passes = (pl.ds(0, grad.shape[1]),)
    chunk = shard * inner
    per_half = outer // 2
    up, down = row + 1 < outer, row >= 1
    east, west = col + 1 < inner, col >= 1
    exists = (up, down, east, west)
    target = (me + inner, me - inner, me + 1, me - 1)

    def rows_of(index):
        return pl.ds(pl.multiple_of(index * shard, shard), shard)

    def shard_copy(turn, index, way, own=False):
        place = grad_v.at[rows_of(index), passes[turn]]
        return pltpu.make_async_remote_copy(
            src_ref=grad.at[:, passes[turn]] if own else place, dst_ref=place,
            send_sem=send_sem.at[turn, way, index], recv_sem=recv_sem.at[turn, index],
            device_id={"gx": target[way]}, device_id_type=MESH)

    def wait_shard(turn, index):
        place = grad_v.at[rows_of(index), passes[turn]]
        pltpu.make_async_remote_copy(
            src_ref=place, dst_ref=place, send_sem=send_sem.at[turn, 0, index], recv_sem=recv_sem.at[turn, index],
            device_id={"gx": me}, device_id_type=MESH).wait_recv()

    def send(turn, index, way, own=False):
        @pl.when(exists[way])
        def _():
            shard_copy(turn, index, way, own).start()

    def pass_on(turn, far):
        @pl.when(row >= far)
        def _():
            index = (row - far) * inner + col
            wait_shard(turn, index)
            for way in (0, 2, 3):
                send(turn, index, way)

        @pl.when(row + far < outer)
        def _():
            index = (row + far) * inner + col
            wait_shard(turn, index)
            for way in (1, 2, 3):
                send(turn, index, way)

    def finish_chunk(turn, c):
        @pl.loop(1, inner)
        def _(e):
            @pl.when(col >= e)
            def _():
                index = c * inner + col - e
                wait_shard(turn, index)
                send(turn, index, 2)

            @pl.when(col + e < inner)
            def _():
                index = c * inner + col + e
                wait_shard(turn, index)
                send(turn, index, 3)

    def weight_copy(n):
        rows = pl.ds(pl.multiple_of(n * tile, tile), tile)
        return pltpu.make_async_copy(weight.at[rows], weight_v.at[rows], weight_sem.at[n])

    barrier = pltpu.get_barrier_semaphore()
    for way in range(4):
        @pl.when(exists[way])
        def _():
            pl.semaphore_signal(barrier, inc=1, device_id={"gx": target[way]}, device_id_type=MESH)
    pl.semaphore_signal(barrier, inc=1, device_id={"gy": peer}, device_id_type=MESH)
    count = 1 + sum(jnp.where(e, 1, 0) for e in exists)
    pl.semaphore_wait(barrier, count)

    for way in (2, 3, 0, 1):
        send(0, me, way, True)
    own = pltpu.make_async_copy(grad, grad_v.at[rows_of(me)], own_sem)
    own.start()

    def pre_copy(n):
        cols = pl.ds(pl.multiple_of(n * small, small), small)
        return pltpu.make_async_copy(preact.at[:, cols], pre_v.at[n % 2], pre_sem.at[n % 2])

    pre_copy(0).start()

    own_rows = pl.ds(pl.multiple_of(core * half, half), half)

    def act_copies(n):
        cols = pl.ds(pl.multiple_of(n * small, small), small)
        here = pltpu.make_async_copy(act_v.at[n % 2], act_out.at[own_rows, cols], act_sem.at[n % 2])
        slope = pltpu.make_async_copy(slope_v.at[n % 2], slope_out.at[:, cols], slope_sem.at[n % 2])
        return here, slope

    def act_exchange(n):
        place = act_out.at[own_rows, pl.ds(pl.multiple_of(n * small, small), small)]
        return pltpu.make_async_remote_copy(
            src_ref=place, dst_ref=place, send_sem=act_send.at[n], recv_sem=act_recv.at[n],
            device_id={"gy": peer}, device_id_type=MESH)

    def drain_act(n):
        for copy in act_copies(n):
            copy.wait()
        act_exchange(n).start()

    @pl.loop(0, smalls)
    def _(n):
        pre_copy(n).wait()

        @pl.when(n + 1 < smalls)
        def _():
            pre_copy(n + 1).start()

        @pl.when(n >= 2)
        def _():
            drain_act(n - 2)

        @pl.loop(0, half // 32)
        def _(s):
            strip = pl.ds(pl.multiple_of(s * 32, 32), 32)
            values = pre_v[n % 2, strip, :].astype(jnp.float32)
            cumulative = 0.5 * (1.0 + lax.erf(values * 0.7071067811865476))
            density = jnp.exp(-0.5 * values * values) * 0.3989422804014327
            act_v[n % 2, strip, :] = (values * cumulative).astype(jnp.bfloat16)
            slope_v[n % 2, strip, :] = cumulative + values * density

        for copy in act_copies(n):
            copy.start()

    @pl.loop(max(smalls - 2, 0), smalls)
    def _(n):
        drain_act(n)

    @pl.loop(0, tiles)
    def _(n):
        weight_copy(n).start()

    own.wait()

    near = jnp.minimum(row, outer - 1 - row)

    def chunk_at(k):
        zigzag = jnp.where(k % 2 == 1, row - (k + 1) // 2, row + k // 2)
        rest = jnp.where(row <= outer - 1 - row, k, outer - 1 - k)
        return jnp.where(k <= 2 * near, zigzag, rest)

    def grad_back(c):
        rows = pl.ds(pl.multiple_of(c * chunk, chunk), chunk)
        return pltpu.make_async_copy(grad_v.at[rows], grad_out.at[rows], out_sem.at[c])

    def part_place(k, n):
        c = chunk_at(k)
        rows = pl.ds(pl.multiple_of(c % per_half * chunk, chunk), chunk)
        return c // per_half == core, rows, pl.ds(pl.multiple_of(n * tile, tile), tile)

    def to_own(step, rows, cols):
        slot = step % STAGES
        return pltpu.make_async_copy(part_v.at[slot], part_own.at[rows, cols], part_sem.at[slot])

    def to_peer(step, rows, cols):
        slot = step % STAGES
        return pltpu.make_async_remote_copy(
            src_ref=part_v.at[slot], dst_ref=part_peer.at[rows, cols],
            send_sem=part_send.at[slot], recv_sem=part_recv,
            device_id={"gy": peer}, device_id_type=MESH)

    def drain(step):
        mine, rows, cols = part_place(step // tiles, step % tiles)

        @pl.when(mine)
        def _():
            to_own(step, rows, cols).wait()

        @pl.when(jnp.logical_not(mine))
        def _():
            to_peer(step, rows, cols).wait_send()

    @pl.loop(0, outer)
    def _(k):
        pass_on(0, k + 1)
        c = chunk_at(k)
        finish_chunk(0, c)
        grad_back(c).start()
        token_rows = pl.ds(pl.multiple_of(c * chunk, chunk), chunk)

        @pl.loop(0, tiles)
        def _(n):
            step = k * tiles + n

            @pl.when(k == 0)
            def _():
                weight_copy(n).wait()

            @pl.when(step >= STAGES)
            def _():
                drain(step - STAGES)

            part = lax.dot_general(
                grad_v[token_rows, :], weight_v[pl.ds(pl.multiple_of(n * tile, tile), tile), :],
                (((1,), (1,)), ((), ())), preferred_element_type=jnp.float32)
            part_v[step % STAGES] = part.astype(jnp.bfloat16)
            mine, rows, cols = part_place(k, n)

            @pl.when(mine)
            def _():
                to_own(step, rows, cols).start()

            @pl.when(jnp.logical_not(mine))
            def _():
                to_peer(step, rows, cols).start()

    @pl.loop(outer * tiles - STAGES, outer * tiles)
    def _(step):
        drain(step)

    @pl.loop(0, smalls)
    def _(n):
        act_exchange(n).wait()

    @pl.loop(0, outer)
    def _(c):
        grad_back(c).wait()
        line = c * inner + col

        for turn in range(1):
            @pl.when(jnp.logical_and(up, c <= row))
            def _():
                shard_copy(turn, line, 0).wait_send()

            @pl.when(jnp.logical_and(down, c >= row))
            def _():
                shard_copy(turn, line, 1).wait_send()

            @pl.loop(0, inner)
            def _(e):
                @pl.when(jnp.logical_and(east, e <= col))
                def _():
                    shard_copy(turn, c * inner + e, 2).wait_send()

                @pl.when(jnp.logical_and(west, e >= col))
                def _():
                    shard_copy(turn, c * inner + e, 3).wait_send()

    pltpu.make_async_remote_copy(
        src_ref=part_peer, dst_ref=part_peer, send_sem=part_send.at[0], recv_sem=part_recv,
        device_id={"gy": peer}, device_id_type=MESH).wait_recv()


def gather_call(inner, parts, preact, grad, weight):
    half, hidden = preact.shape
    shard, features = grad.shape
    outer = parts // inner
    tile, small = pick_tile(hidden, 1024), pick_tile(hidden, 256)
    tokens = shard * parts
    any_spec = pl.BlockSpec(memory_space=pl.ANY)
    return pl.pallas_call(
        functools.partial(gather_kernel, outer, inner, tile, small),
        out_shape=(
            jax.ShapeDtypeStruct((tokens, hidden), jnp.bfloat16),
            jax.ShapeDtypeStruct((half, hidden), jnp.float32),
            jax.ShapeDtypeStruct((tokens, features), jnp.bfloat16),
            jax.ShapeDtypeStruct((half, hidden), jnp.bfloat16),
            jax.ShapeDtypeStruct((half, hidden), jnp.bfloat16),
        ),
        in_specs=[any_spec] * 3,
        out_specs=(any_spec,) * 5,
        scratch_shapes=[
            pltpu.VMEM((hidden, features), jnp.bfloat16),
            pltpu.VMEM((tokens, features), jnp.bfloat16),
            pltpu.VMEM((2, half, small), jnp.bfloat16),
            pltpu.VMEM((2, half, small), jnp.bfloat16),
            pltpu.VMEM((2, half, small), jnp.float32),
            pltpu.VMEM((STAGES, shard * inner, tile), jnp.bfloat16),
            pltpu.SemaphoreType.DMA((hidden // tile,)),
            pltpu.SemaphoreType.DMA,
            pltpu.SemaphoreType.DMA((outer,)),
            pltpu.SemaphoreType.DMA((1, 4, parts)),
            pltpu.SemaphoreType.DMA((1, parts)),
            pltpu.SemaphoreType.DMA((2,)),
            pltpu.SemaphoreType.DMA((2,)),
            pltpu.SemaphoreType.DMA((2,)),
            pltpu.SemaphoreType.DMA((hidden // small,)),
            pltpu.SemaphoreType.DMA((hidden // small,)),
            pltpu.SemaphoreType.DMA((STAGES,)),
            pltpu.SemaphoreType.DMA((STAGES,)),
            pltpu.SemaphoreType.DMA,
        ],
        compiler_params=pltpu.CompilerParams(
            collective_id=0, has_side_effects=True, vmem_limit_bytes=VMEM_BYTES),
        cost_estimate=pl.CostEstimate(
            flops=2 * tokens * hidden * features, bytes_accessed=2 * hidden * features,
            transcendentals=half * hidden),
        name="gather_hidden_grad",
    )(preact, grad, weight)


def weight_kernel(act, grad, slope, part_own, part_peer, weight_grad, preact_grad):
    turned = act[...].T
    rest = grad.shape[1]
    for start in range(0, rest, 1024):
        stop = min(start + 1024, rest)
        weight_grad[:, start:stop] = jnp.dot(
            turned, grad[:, start:stop], preferred_element_type=jnp.float32).astype(jnp.bfloat16)
    for start in range(0, slope.shape[0], 32):
        strip = slice(start, start + 32)
        total = part_own[strip, :].astype(jnp.float32) + part_peer[strip, :].astype(jnp.float32)
        preact_grad[strip, :] = (total * slope[strip, :]).astype(jnp.bfloat16)


def weight_call(act, slope, grad, part_own, part_peer):
    tokens, hidden = act.shape
    features = grad.shape[1]
    half = slope.shape[0]
    tile = pick_tile(hidden, 512)
    block = pl.BlockSpec((half, tile), lambda i: (0, i))
    return pl.pallas_call(
        weight_kernel,
        grid=(hidden // tile,),
        out_shape=(
            jax.ShapeDtypeStruct((hidden, features), jnp.bfloat16),
            jax.ShapeDtypeStruct((half, hidden), jnp.bfloat16),
        ),
        in_specs=[
            pl.BlockSpec((tokens, tile), lambda i: (0, i)),
            pl.BlockSpec((tokens, features), lambda i: (0, 0), pipeline_mode=pl.Buffered(1)),
            block, block, block,
        ],
        out_specs=(pl.BlockSpec((tile, features), lambda i: (i, 0)), block),
        compiler_params=pltpu.CompilerParams(vmem_limit_bytes=VMEM_BYTES),
        cost_estimate=pl.CostEstimate(
            flops=2 * tokens * hidden * features, bytes_accessed=4 * hidden * features, transcendentals=0),
        name="weight_grad",
    )(act, grad, slope, part_own, part_peer)


def solution(mesh):
    parts = mesh.shape["gx"]
    inner = 2 ** ((parts.bit_length() - 1) // 2)

    def body(saved_preact, output_grad, down_weight):
        act, slope, grad, part_own, part_peer = gather_call(
            inner, parts, saved_preact, output_grad, down_weight)
        weight_grad, preact_grad = weight_call(act, slope, grad, part_own, part_peer)
        return preact_grad, weight_grad

    return jax.shard_map(
        body,
        mesh=mesh,
        in_specs=(P(("groups", "gy"), "gx"), P(("groups", "gx"), "gy"), P("gx", "gy")),
        out_specs=(P(("groups", "gy"), "gx"), P(("groups", "gx"), "gy")),
        check_vma=False,
    )
```

time: 180 us -> 170 us (0.944)
  Pallas kernels: 179 us -> 169 us
    pallas_call x1, Pallas kernels: 66.4 us -> 59.5 us  [weight_call(): pl.pallas_call(weight_kernel, grid=(hidden // tile,), out_shape=(jax.Shap...]
    pallas_call x1, Pallas kernels: 112 us -> 109 us  [gather_call(): pl.pallas_call(functools.partial(gather_kernel, outer, inner, tile, small...]
where the time goes in v2:
time: 170 us; the launch traced here: 169 us
  Pallas kernels  169 us (99%)
    pallas_call x1, Pallas kernels, gather_call(): pl.pallas_call(functools.partial(gather_kernel, outer, inner, tile, small...  109 us
    pallas_call x1, Pallas kernels, weight_call(): pl.pallas_call(weight_kernel, grid=(hidden // tile,), out_shape=(jax.Shap...  59.5 us

profile of v2, /device:TPU:0, one launch (start us, length us, event | category | flops | bytes accessed | tf_op | source)
XLA Modules:
  0.0 169.2 jit_solution(14499140120773524787)
XLA Ops:
  0.6 109.1 %gather_hidden_grad.1 = (bf16[1024,6144]{1,0:T(8,128)(2,1)}, f32[512,6144]{1,0:T(8,128)}, bf16[1024,3712]{1,0:T(8,128)(2,1)}, bf16[512,6144]{1,0:T(8,128)(2,1)}, bf16[512,6144]{1,0:T(8,128)(2,1)}) custom-call(bf16[512,6144]{1,0:T(8,128)(2,1)} %preact.1, bf16[128,3712]{1,0:T(8,128)(2,1)} %grad.1, bf16[6144,3712]{1,0:T(8,128)(2,1)} %weight.1), custom_call_target="tpu_custom_call" | custom-call | flops 46707769344 | bytes 45613056 | tf_op jit(solution)/shard_map/gather_hidden_grad/pallas_call | solution.py:282
  109.7 59.5 %weight_grad.1 = (bf16[6144,3712]{1,0:T(8,128)(2,1)}, bf16[512,6144]{1,0:T(8,128)(2,1)}) custom-call(bf16[1024,6144]{1,0:T(8,128)(2,1)} %get-tuple-element.9.act, bf16[1024,3712]{1,0:T(8,128)(2,1)} %get-tuple-element.10.grad, f32[512,6144]{1,0:T(8,128)} %get-tuple-element.11.slope, bf16[512,6144]{1,0:T(8,128)(2,1)} %get-tuple-element.12.part_own, ...), custom_call_target="tpu_custom_call" | custom-call | flops 46707769344 | bytes 91226112 | tf_op jit(solution)/shard_map/weight_grad/pallas_call | solution.py:342
